TPU v7x, 32 devices: a whole 2x2x4 slice. The times are simulated.
32 devices in a mesh: gx: 8 (over z, core), gy: 4 (over y, x).
Axes of the slice: x: 2, y: 2, z: 4, core: 2. Of those that a mesh axis runs over, the one named last changes fastest.
Arguments:
- payload: float32 [4, 524288], P(None, ('gx', 'gy'))
- cells: int32 [3, 524288], P(None, ('gx', 'gy')), may hold values from 0 to 127, as said below
- counts: int32 [32, 9], P(('gx', 'gy')), may hold values from 128 to 12596, as said below
Outputs:
- scalar_field: float32 [8, 128, 512], P(None, 'gx', 'gy')
- momentum: float32 [3, 8, 128, 512], P(None, None, 'gx', 'gy')
Inputs may be any that keep to these rules, and one draw needn't show every extreme that they name: Rows of a tile are grouped by direction in the order of counts' columns. A face direction holds at most 2048 rows of a tile and a corner direction at most 512; each of these bounds is reached in some tile. A row of counts sums to 16384. cells[0] is below 8, cells[1] below 16, cells[2] below 128. A particle moving +x lands in x layers 0 to 1 of its destination tile, one moving -x in layers 14 to 15; likewise +y in y layers 0 to 15 and -y in 112 to 127; corner directions are bound in both; otherwise any cell.
All inputs are finite; a program needn't handle non-finite values.
Results may differ from a plain program's by a relative error of at most 0.000054.
Values sent between devices are 32-bit elements; how exact they have to be, the bound alone decides.
A program may use at most 64 MiB of HBM per device.

v0:
```python
import jax
import jax.numpy as jnp
from jax import lax
from jax.sharding import PartitionSpec as P

CX = 16
CY = 128
NZ = 8
SWEEPS = 4
PART = 16384
CAP_F = 2048
MX = 2
MY = 16


SCREENING = 0.5
CUBIC_TERM = 0.3
COUPLING = 1.5
SMOOTHING = 0.1
BACKGROUND = 1.0


def from_behind(block, axis, distance):
    devices = range(lax.axis_size(axis))
    route = [((i - distance) % len(devices), i) for i in devices]
    return lax.ppermute(block, axis, route)


def extended_2(cells, sides, width):
    for axis, dim in sides:
        count = lax.axis_size(axis)
        head = lax.slice_in_dim(cells, 0, width, axis=dim)
        tail = lax.slice_in_dim(cells, cells.shape[dim] - width, cells.shape[dim], axis=dim)
        cells = jnp.concatenate(
            [
                lax.ppermute(tail, axis, [(i, (i + 1) % count) for i in range(count)]),
                cells,
                lax.ppermute(head, axis, [((i + 1) % count, i) for i in range(count)]),
            ],
            axis=dim,
        )
    return cells


def direction_steps(direction):
    step_x = ((direction == 0) | (direction == 4) | (direction == 5)).astype(jnp.int32) - (
        (direction == 1) | (direction == 6) | (direction == 7)
    ).astype(jnp.int32)
    step_y = ((direction == 2) | (direction == 4) | (direction == 6)).astype(jnp.int32) - (
        (direction == 3) | (direction == 5) | (direction == 7)
    ).astype(jnp.int32)
    return (step_x, step_y)


def deposit(payload, row_index, col_index, width_rows, width_cols, block):
    masses = payload[0]
    values = jnp.concatenate([masses[None, :], masses[None, :] * payload[1:]], axis=0)
    turns = values.shape[1] // block
    value_blocks = jnp.transpose(values.reshape(4, turns, block), (1, 0, 2))
    row_blocks = row_index.reshape(turns, block)
    col_blocks = col_index.reshape(turns, block)
    row_ids = lax.broadcasted_iota(jnp.int32, (1, width_rows), 1)
    col_ids = lax.broadcasted_iota(jnp.int32, (1, 1, width_cols), 2)

    def add_block(total, pieces):
        value_part, row_part, col_part = pieces
        left_hot = (row_part[:, None] == row_ids).astype(jnp.float32)
        right_hot = (col_part[:, None, None] == col_ids).astype(jnp.float32) * jnp.transpose(
            value_part
        )[:, :, None]
        right_hot = right_hot.reshape(block, 4 * width_cols)
        product = lax.dot_general(
            left_hot,
            right_hot,
            (((0,), (0,)), ((), ())),
            precision=lax.Precision.HIGHEST,
            preferred_element_type=jnp.float32,
        )
        return (total + product, None)

    start = jnp.zeros((width_rows, 4 * width_cols), jnp.float32)
    total, unused = lax.scan(add_block, start, (value_blocks, row_blocks, col_blocks))
    return jnp.transpose(total.reshape(width_rows, 4, width_cols), (1, 0, 2))


def neighbours(bordered):
    middle = bordered[:, 1:-1, 1:-1]
    stacked = jnp.pad(middle, ((1, 1), (0, 0), (0, 0)))
    return (
        stacked[2:]
        + stacked[:-2]
        + bordered[:, 2:, 1:-1]
        + bordered[:, :-2, 1:-1]
        + bordered[:, 1:-1, 2:]
        + bordered[:, 1:-1, :-2]
    )


def smooth_source(bordered):
    middle = bordered[:, 1:-1, 1:-1]
    smoothed = middle + SMOOTHING * (neighbours(bordered) - 6.0 * middle)
    return COUPLING * (smoothed - BACKGROUND)


def relax_cells(bordered, source, parity, colour):
    middle = bordered[:, 1:-1, 1:-1]
    residual = (
        neighbours(bordered)
        - 6.0 * middle
        - SCREENING * middle
        - CUBIC_TERM * middle * middle * middle
        - source
    )
    slope = -6.0 - SCREENING - 3.0 * CUBIC_TERM * middle * middle
    return jnp.where(parity == colour, middle - residual / slope, middle)


def parity_of(width_x, width_y):
    total = (
        lax.broadcasted_iota(jnp.int32, (NZ, width_x, width_y), 0)
        + lax.broadcasted_iota(jnp.int32, (NZ, width_x, width_y), 1)
        + lax.broadcasted_iota(jnp.int32, (NZ, width_x, width_y), 2)
    )
    return total % 2


def shards(payload, cells, counts):
    tallies = counts[0]
    limits = jnp.cumsum(tallies)
    position = jnp.arange(PART, dtype=jnp.int32)
    direction = jnp.zeros((PART,), jnp.int32)
    for edge in range(8):
        direction = direction + (position >= limits[edge]).astype(jnp.int32)
    step_x, step_y = direction_steps(direction)
    extent_x = CX + 2 * MX
    extent_y = CY + 2 * MY
    row_index = cells[0] * extent_x + cells[1] + MX + step_x * CX
    col_index = cells[2] + MY + step_y * CY
    extended = deposit(payload, row_index, col_index, NZ * extent_x, extent_y, CAP_F)
    extended = extended.reshape(4, NZ, extent_x, extent_y)
    from_left = from_behind(extended[:, :, CX + MX :, :], "gx", 1)
    from_right = from_behind(extended[:, :, :MX, :], "gx", -1)
    central = extended[:, :, MX : MX + CX, :]
    central = central.at[:, :, :MX, :].add(from_left).at[:, :, CX - MX :, :].add(from_right)
    from_below = from_behind(central[:, :, :, CY + MY :], "gy", 1)
    from_above = from_behind(central[:, :, :, :MY], "gy", -1)
    interior = central[:, :, :, MY : MY + CY]
    interior = interior.at[:, :, :, :MY].add(from_below).at[:, :, :, CY - MY :].add(from_above)
    density = interior[0]
    momentum = interior[1:]
    scalar_field = jnp.zeros((NZ, CX, CY), jnp.float32)
    parity_core = parity_of(CX, CY)
    padded = extended_2(density, (("gx", 1), ("gy", 2)), 1)
    source = smooth_source(padded)
    for sweep_no in range(SWEEPS):
        for colour in (0, 1):
            bordered = extended_2(scalar_field, (("gx", 1), ("gy", 2)), 1)
            scalar_field = relax_cells(bordered, source, parity_core, colour)
    return (scalar_field, momentum)


def solution(mesh):
    placed = (P(None, ("gx", "gy")), P(None, ("gx", "gy")), P(("gx", "gy"), None))
    return jax.shard_map(
        shards,
        mesh=mesh,
        in_specs=placed,
        out_specs=(P(None, "gx", "gy"), P(None, None, "gx", "gy")),
        check_vma=False,
    )
```

profile of v0, /device:TPU:0, one launch (start us, length us, event | category | flops | bytes accessed | tf_op | source)
XLA Modules:
  0.0 230.9 jit_solution(7122601879521464910)
XLA Ops:
  2.2 1.7 add_reduce_fusion
  4.9 1.1 slice_multiply_fusion
  6.1 5.2 %multiply_add_fusion = (s32[8,2048]{1,0:T(8,128)S(1)}, s32[8,2048]{1,0:T(8,128)S(1)}) fusion(s32[8,2048]{1,0:T(8,128)S(1)} %add.347, s32[]{:T(128)} %bitcast.8, s32[]{:T(128)} %bitcast.7, s32[]{:T(128)} %bitcast.6, s32[]{:T(128)} %bitcast.5, s32[]{:T(128)} %bitcast.4, s32[]{:T(128)} %bitcast.3, s32[]{:T(128)} %bitcast.2, s32[]{:T(128)} %bitcast.1, ...), kind=kLoop, calls=%fused_computation.240 | loop fusion | flops 835584 | bytes 262176 | tf_op jit(solution)/shard_map/add | solution.py:138
  11.2 74.9 %while.15 = (s32[]{:T(128)}, f32[160,640]{1,0:T(8,128)S(1)}, s32[8,2048]{1,0:T(8,128)S(1)}, s32[8,2048]{1,0:T(8,128)S(1)}, f32[8,4,2048]{2,1,0:T(4,128)S(1)}, /*index=5*/s32[]{:T(128)}, s32[]{:T(128)}) while((s32[]{:T(128)}, f32[160,640]{1,0:T(8,128)S(1)}, s32[8,2048]{1,0:T(8,128)S(1)}, s32[8,2048]{1,0:T(8,128)S(1)}, ...), condition=%wide.region_2.3_spmd.clone, body=%wide.region_1.2_spmd.clone.sunk | while | flops 2519408640 | bytes 14073951 | solution.py:82
  11.4 3.0 %broadcast_multiply_fusion.2 = f32[2048,4,160]{0,2,1:T(8,128)} fusion(f32[2048,4]{0,1:T(4,128)S(1)} %dynamic-slice_bitcast_fusion.2, f32[2048,160]{0,1:T(8,128)S(1)} %fusion.144), kind=kLoop, calls=%fused_computation.2.clone.1 | loop fusion | flops 1310720 | bytes 6586368 | tf_op jit(solution)/shard_map/while/body/eval_jaxpr/mul | solution.py:68
  14.4 6.2 %convolution_add_fusion.2 = f32[160,640]{1,0:T(8,128)S(1)} fusion(f32[2048,640]{0,1:T(8,128)} %bitcast.35, s32[2048]{0:T(1024)S(1)} %bitcast.39, f32[160,640]{1,0:T(8,128)S(1)} %get-tuple-element.219, pred[]{:T(512)S(6)} %compare.37), kind=kOutput, calls=%fused_computation.7.clone.1 | convolution fusion | flops 2517442560 | bytes 6070273 | tf_op jit(solution)/shard_map/while/body/eval_jaxpr/dot_general | solution.py:72
  20.8 3.0 %broadcast_multiply_fusion.2 = f32[2048,4,160]{0,2,1:T(8,128)} fusion(f32[2048,4]{0,1:T(4,128)S(1)} %dynamic-slice_bitcast_fusion.2, f32[2048,160]{0,1:T(8,128)S(1)} %fusion.144), kind=kLoop, calls=%fused_computation.2.clone.1 | loop fusion | flops 1310720 | bytes 6586368 | tf_op jit(solution)/shard_map/while/body/eval_jaxpr/mul | solution.py:68
  23.8 6.2 %convolution_add_fusion.2 = f32[160,640]{1,0:T(8,128)S(1)} fusion(f32[2048,640]{0,1:T(8,128)} %bitcast.35, s32[2048]{0:T(1024)S(1)} %bitcast.39, f32[160,640]{1,0:T(8,128)S(1)} %get-tuple-element.219, pred[]{:T(512)S(6)} %compare.37), kind=kOutput, calls=%fused_computation.7.clone.1 | convolution fusion | flops 2517442560 | bytes 6070273 | tf_op jit(solution)/shard_map/while/body/eval_jaxpr/dot_general | solution.py:72
  30.2 3.0 %broadcast_multiply_fusion.2 = f32[2048,4,160]{0,2,1:T(8,128)} fusion(f32[2048,4]{0,1:T(4,128)S(1)} %dynamic-slice_bitcast_fusion.2, f32[2048,160]{0,1:T(8,128)S(1)} %fusion.144), kind=kLoop, calls=%fused_computation.2.clone.1 | loop fusion | flops 1310720 | bytes 6586368 | tf_op jit(solution)/shard_map/while/body/eval_jaxpr/mul | solution.py:68
  33.1 6.2 %convolution_add_fusion.2 = f32[160,640]{1,0:T(8,128)S(1)} fusion(f32[2048,640]{0,1:T(8,128)} %bitcast.35, s32[2048]{0:T(1024)S(1)} %bitcast.39, f32[160,640]{1,0:T(8,128)S(1)} %get-tuple-element.219, pred[]{:T(512)S(6)} %compare.37), kind=kOutput, calls=%fused_computation.7.clone.1 | convolution fusion | flops 2517442560 | bytes 6070273 | tf_op jit(solution)/shard_map/while/body/eval_jaxpr/dot_general | solution.py:72
  39.5 3.0 %broadcast_multiply_fusion.2 = f32[2048,4,160]{0,2,1:T(8,128)} fusion(f32[2048,4]{0,1:T(4,128)S(1)} %dynamic-slice_bitcast_fusion.2, f32[2048,160]{0,1:T(8,128)S(1)} %fusion.144), kind=kLoop, calls=%fused_computation.2.clone.1 | loop fusion | flops 1310720 | bytes 6586368 | tf_op jit(solution)/shard_map/while/body/eval_jaxpr/mul | solution.py:68
  42.5 6.2 %convolution_add_fusion.2 = f32[160,640]{1,0:T(8,128)S(1)} fusion(f32[2048,640]{0,1:T(8,128)} %bitcast.35, s32[2048]{0:T(1024)S(1)} %bitcast.39, f32[160,640]{1,0:T(8,128)S(1)} %get-tuple-element.219, pred[]{:T(512)S(6)} %compare.37), kind=kOutput, calls=%fused_computation.7.clone.1 | convolution fusion | flops 2517442560 | bytes 6070273 | tf_op jit(solution)/shard_map/while/body/eval_jaxpr/dot_general | solution.py:72
  48.9 3.0 %broadcast_multiply_fusion.2 = f32[2048,4,160]{0,2,1:T(8,128)} fusion(f32[2048,4]{0,1:T(4,128)S(1)} %dynamic-slice_bitcast_fusion.2, f32[2048,160]{0,1:T(8,128)S(1)} %fusion.144), kind=kLoop, calls=%fused_computation.2.clone.1 | loop fusion | flops 1310720 | bytes 6586368 | tf_op jit(solution)/shard_map/while/body/eval_jaxpr/mul | solution.py:68
  51.9 6.2 %convolution_add_fusion.2 = f32[160,640]{1,0:T(8,128)S(1)} fusion(f32[2048,640]{0,1:T(8,128)} %bitcast.35, s32[2048]{0:T(1024)S(1)} %bitcast.39, f32[160,640]{1,0:T(8,128)S(1)} %get-tuple-element.219, pred[]{:T(512)S(6)} %compare.37), kind=kOutput, calls=%fused_computation.7.clone.1 | convolution fusion | flops 2517442560 | bytes 6070273 | tf_op jit(solution)/shard_map/while/body/eval_jaxpr/dot_general | solution.py:72
  58.2 3.0 %broadcast_multiply_fusion.2 = f32[2048,4,160]{0,2,1:T(8,128)} fusion(f32[2048,4]{0,1:T(4,128)S(1)} %dynamic-slice_bitcast_fusion.2, f32[2048,160]{0,1:T(8,128)S(1)} %fusion.144), kind=kLoop, calls=%fused_computation.2.clone.1 | loop fusion | flops 1310720 | bytes 6586368 | tf_op jit(solution)/shard_map/while/body/eval_jaxpr/mul | solution.py:68
  61.2 6.2 %convolution_add_fusion.2 = f32[160,640]{1,0:T(8,128)S(1)} fusion(f32[2048,640]{0,1:T(8,128)} %bitcast.35, s32[2048]{0:T(1024)S(1)} %bitcast.39, f32[160,640]{1,0:T(8,128)S(1)} %get-tuple-element.219, pred[]{:T(512)S(6)} %compare.37), kind=kOutput, calls=%fused_computation.7.clone.1 | convolution fusion | flops 2517442560 | bytes 6070273 | tf_op jit(solution)/shard_map/while/body/eval_jaxpr/dot_general | solution.py:72
  67.6 3.0 %broadcast_multiply_fusion.2 = f32[2048,4,160]{0,2,1:T(8,128)} fusion(f32[2048,4]{0,1:T(4,128)S(1)} %dynamic-slice_bitcast_fusion.2, f32[2048,160]{0,1:T(8,128)S(1)} %fusion.144), kind=kLoop, calls=%fused_computation.2.clone.1 | loop fusion | flops 1310720 | bytes 6586368 | tf_op jit(solution)/shard_map/while/body/eval_jaxpr/mul | solution.py:68
  70.6 6.2 %convolution_add_fusion.2 = f32[160,640]{1,0:T(8,128)S(1)} fusion(f32[2048,640]{0,1:T(8,128)} %bitcast.35, s32[2048]{0:T(1024)S(1)} %bitcast.39, f32[160,640]{1,0:T(8,128)S(1)} %get-tuple-element.219, pred[]{:T(512)S(6)} %compare.37), kind=kOutput, calls=%fused_computation.7.clone.1 | convolution fusion | flops 2517442560 | bytes 6070273 | tf_op jit(solution)/shard_map/while/body/eval_jaxpr/dot_general | solution.py:72
  77.0 3.0 %broadcast_multiply_fusion.2 = f32[2048,4,160]{0,2,1:T(8,128)} fusion(f32[2048,4]{0,1:T(4,128)S(1)} %dynamic-slice_bitcast_fusion.2, f32[2048,160]{0,1:T(8,128)S(1)} %fusion.144), kind=kLoop, calls=%fused_computation.2.clone.1 | loop fusion | flops 1310720 | bytes 6586368 | tf_op jit(solution)/shard_map/while/body/eval_jaxpr/mul | solution.py:68
  80.0 6.2 %convolution_add_fusion.2 = f32[160,640]{1,0:T(8,128)S(1)} fusion(f32[2048,640]{0,1:T(8,128)} %bitcast.35, s32[2048]{0:T(1024)S(1)} %bitcast.39, f32[160,640]{1,0:T(8,128)S(1)} %get-tuple-element.219, pred[]{:T(512)S(6)} %compare.37), kind=kOutput, calls=%fused_computation.7.clone.1 | convolution fusion | flops 2517442560 | bytes 6070273 | tf_op jit(solution)/shard_map/while/body/eval_jaxpr/dot_general | solution.py:72
  87.2 4.1 %collective-permute-start = (f32[8,1,128]{2,1,0:T(1,128)S(1)}, f32[8,1,128]{2,1,0:T(1,128)S(1)}, u32[]{:S(2)}, u32[]{:S(2)}) collective-permute-start(f32[8,1,128]{2,1,0:T(1,128)S(1)} %broadcast.243), channel_id=1, source_target_pairs={{4,0},{8,4},{12,8},{16,12},{20,16},{24,20},{28,24},{0,28},{5,1},{9... | collective-permute-start | bytes 12296 | tf_op jit(solution)/shard_map/ppermute | solution.py:38
  91.3 3.5 %collective-permute-start.5 = (f32[4,8,2,160]{3,0,2,1:T(4,128)S(1)}, f32[4,8,2,160]{3,0,2,1:T(4,128)S(1)}, u32[]{:S(2)}, u32[]{:S(2)}) collective-permute-start(f32[4,8,2,160]{3,0,2,1:T(4,128)S(1)} %get-tuple-element.128), channel_id=1, source_target_pairs={{4,0},{8,4},{12,8},{16,12},{20,16},{24,20},{28,24},{0,28},{5,1},{9... | collective-permute-start | bytes 122888 | tf_op jit(solution)/shard_map/ppermute | solution.py:26
  94.9 1.8 collective-permute-done.5
  96.9 2.0 collective-permute-start.6
  99.2 1.1 collective-permute-start.7
  100.2 6.9 %collective-permute-done.6 = f32[4,8,16,16]{3,0,2,1:T(4,128)S(1)} collective-permute-done((f32[4,8,16,16]{3,0,2,1:T(4,128)S(1)}, f32[4,8,16,16]{3,0,2,1:T(4,128)S(1)}, u32[]{:S(2)}, u32[]{:S(2)}) %collective-permute-start.6) | collective-permute-done | bytes 32800 | tf_op jit(solution)/shard_map/ppermute | solution.py:26
  107.3 4.0 %scatter-add.16 = f32[4,8,16,128]{3,0,2,1:T(4,128)S(1)} dynamic-update-slice(f32[4,8,16,128]{3,0,2,1:T(4,128)S(1)} %slice.609, f32[4,8,16,16]{3,0,2,1:T(4,128)S(1)} %slice_add_fusion.1, s32[]{:T(128)} %constant.174.clone.1, s32[]{:T(128)} %constant.174.clone.1, s32[]{:T(128)} %constant.174.clone.1, s32[]{:T(128)} %constant.174.clone.1) | dynamic-update-slice | bytes 65540 | tf_op jit(solution)/shard_map/scatter-add | solution.py:148
  111.5 21.2 %scatter-add.19 = f32[4,8,16,128]{3,0,2,1:T(4,128)S(1)} dynamic-update-slice(f32[4,8,16,128]{3,0,2,1:T(4,128)S(1)} %scatter-add.16, f32[4,8,16,16]{3,0,2,1:T(4,128)S(1)} %slice_add_fusion, s32[]{:T(128)} %constant.174.clone.1, s32[]{:T(128)} %constant.174.clone.1, s32[]{:T(128)} %constant.174.clone.1, s32[]{:T(128)} %constant.188.clone.1) | dynamic-update-slice | bytes 65540 | tf_op jit(solution)/shard_map/scatter-add | solution.py:148
  132.8 2.7 %collective-permute-start.8 = (f32[8,1,128]{2,1,0:T(1,128)S(1)}, f32[8,1,128]{2,1,0:T(1,128)S(1)}, u32[]{:S(2)}, u32[]{:S(2)}) collective-permute-start(f32[8,1,128]{2,1,0:T(1,128)S(1)} %get-tuple-element.165), channel_id=1, source_target_pairs={{4,0},{8,4},{12,8},{16,12},{20,16},{24,20},{28,24},{0,28},{5,1},{9... | collective-permute-start | bytes 12296 | tf_op jit(solution)/shard_map/ppermute | solution.py:38
  135.5 1.6 collective-permute-start.2
  137.6 2.7 %collective-permute-done.9 = f32[8,1,128]{2,1,0:T(1,128)S(1)} collective-permute-done((f32[8,1,128]{2,1,0:T(1,128)S(1)}, f32[8,1,128]{2,1,0:T(1,128)S(1)}, u32[]{:S(2)}, u32[]{:S(2)}) %collective-permute-start.9) | collective-permute-done | bytes 4128 | tf_op jit(solution)/shard_map/ppermute | solution.py:36
  140.4 1.6 collective-permute-start.10
  142.4 1.6 collective-permute-done.3
  145.0 2.4 %collective-permute-done.11 = f32[8,18,1]{2,1,0:T(8,128)S(1)} collective-permute-done((f32[8,18,1]{2,1,0:T(8,128)S(1)}, f32[8,18,1]{2,1,0:T(8,128)S(1)}, u32[]{:S(2)}, u32[]{:S(2)}) %collective-permute-start.11) | collective-permute-done | bytes 608 | tf_op jit(solution)/shard_map/ppermute | solution.py:36
  147.7 1.4 collective-permute-start.12
  149.1 1.3 collective-permute-done.12
  150.4 3.5 %collective-permute-done.13 = f32[8,1,128]{2,1,0:T(1,128)S(1)} collective-permute-done((f32[8,1,128]{2,1,0:T(1,128)S(1)}, f32[8,1,128]{2,1,0:T(1,128)S(1)}, u32[]{:S(2)}, u32[]{:S(2)}) %collective-permute-start.13) | collective-permute-done | bytes 4128 | tf_op jit(solution)/shard_map/ppermute | solution.py:36
  154.9 1.2 collective-permute-start.15
  156.1 2.6 %collective-permute-done.14 = f32[8,18,1]{2,1,0:T(8,128)S(1)} collective-permute-done((f32[8,18,1]{2,1,0:T(8,128)S(1)}, f32[8,18,1]{2,1,0:T(8,128)S(1)}, u32[]{:S(2)}, u32[]{:S(2)}) %collective-permute-start.14) | collective-permute-done | bytes 608 | tf_op jit(solution)/shard_map/ppermute | solution.py:38
  158.7 1.7 collective-permute-done.15
  162.0 3.6 %collective-permute-done.17 = f32[8,1,128]{2,1,0:T(1,128)S(1)} collective-permute-done((f32[8,1,128]{2,1,0:T(1,128)S(1)}, f32[8,1,128]{2,1,0:T(1,128)S(1)}, u32[]{:S(2)}, u32[]{:S(2)}) %collective-permute-start.17) | collective-permute-done | bytes 4128 | tf_op jit(solution)/shard_map/ppermute | solution.py:36
  166.5 1.2 collective-permute-start.19
  167.7 2.6 %collective-permute-done.18 = f32[8,18,1]{2,1,0:T(8,128)S(1)} collective-permute-done((f32[8,18,1]{2,1,0:T(8,128)S(1)}, f32[8,18,1]{2,1,0:T(8,128)S(1)}, u32[]{:S(2)}, u32[]{:S(2)}) %collective-permute-start.18) | collective-permute-done | bytes 608 | tf_op jit(solution)/shard_map/ppermute | solution.py:38
  170.3 1.7 collective-permute-done.19
  173.6 3.6 %collective-permute-done.21 = f32[8,1,128]{2,1,0:T(1,128)S(1)} collective-permute-done((f32[8,1,128]{2,1,0:T(1,128)S(1)}, f32[8,1,128]{2,1,0:T(1,128)S(1)}, u32[]{:S(2)}, u32[]{:S(2)}) %collective-permute-start.21) | collective-permute-done | bytes 4128 | tf_op jit(solution)/shard_map/ppermute | solution.py:36
  178.3 1.1 collective-permute-start.23
  179.3 2.6 %collective-permute-done.22 = f32[8,18,1]{2,1,0:T(8,128)S(1)} collective-permute-done((f32[8,18,1]{2,1,0:T(8,128)S(1)}, f32[8,18,1]{2,1,0:T(8,128)S(1)}, u32[]{:S(2)}, u32[]{:S(2)}) %collective-permute-start.22) | collective-permute-done | bytes 608 | tf_op jit(solution)/shard_map/ppermute | solution.py:38
  181.9 1.9 collective-permute-done.23
  185.4 3.6 %collective-permute-done.25 = f32[8,1,128]{2,1,0:T(1,128)S(1)} collective-permute-done((f32[8,1,128]{2,1,0:T(1,128)S(1)}, f32[8,1,128]{2,1,0:T(1,128)S(1)}, u32[]{:S(2)}, u32[]{:S(2)}) %collective-permute-start.25) | collective-permute-done | bytes 4128 | tf_op jit(solution)/shard_map/ppermute | solution.py:36
  189.7 1.5 collective-permute-start.27
  191.1 2.6 %collective-permute-done.26 = f32[8,18,1]{2,1,0:T(8,128)S(1)} collective-permute-done((f32[8,18,1]{2,1,0:T(8,128)S(1)}, f32[8,18,1]{2,1,0:T(8,128)S(1)}, u32[]{:S(2)}, u32[]{:S(2)}) %collective-permute-start.26) | collective-permute-done | bytes 608 | tf_op jit(solution)/shard_map/ppermute | solution.py:38
  193.7 1.5 collective-permute-done.27
  196.7 3.6 %collective-permute-done.29 = f32[8,1,128]{2,1,0:T(1,128)S(1)} collective-permute-done((f32[8,1,128]{2,1,0:T(1,128)S(1)}, f32[8,1,128]{2,1,0:T(1,128)S(1)}, u32[]{:S(2)}, u32[]{:S(2)}) %collective-permute-start.29) | collective-permute-done | bytes 4128 | tf_op jit(solution)/shard_map/ppermute | solution.py:36
  201.3 1.2 collective-permute-start.31
  202.5 2.6 %collective-permute-done.30 = f32[8,18,1]{2,1,0:T(8,128)S(1)} collective-permute-done((f32[8,18,1]{2,1,0:T(8,128)S(1)}, f32[8,18,1]{2,1,0:T(8,128)S(1)}, u32[]{:S(2)}, u32[]{:S(2)}) %collective-permute-start.30) | collective-permute-done | bytes 608 | tf_op jit(solution)/shard_map/ppermute | solution.py:38
  205.1 1.7 collective-permute-done.31
  208.3 3.6 %collective-permute-done.33 = f32[8,1,128]{2,1,0:T(1,128)S(1)} collective-permute-done((f32[8,1,128]{2,1,0:T(1,128)S(1)}, f32[8,1,128]{2,1,0:T(1,128)S(1)}, u32[]{:S(2)}, u32[]{:S(2)}) %collective-permute-start.33) | collective-permute-done | bytes 4128 | tf_op jit(solution)/shard_map/ppermute | solution.py:36
  212.9 1.2 collective-permute-start.35
  214.1 2.6 %collective-permute-done.34 = f32[8,18,1]{2,1,0:T(8,128)S(1)} collective-permute-done((f32[8,18,1]{2,1,0:T(8,128)S(1)}, f32[8,18,1]{2,1,0:T(8,128)S(1)}, u32[]{:S(2)}, u32[]{:S(2)}) %collective-permute-start.34) | collective-permute-done | bytes 608 | tf_op jit(solution)/shard_map/ppermute | solution.py:38
  216.7 1.7 collective-permute-done.35
  219.9 3.6 %collective-permute-done.37 = f32[8,1,128]{2,1,0:T(1,128)S(1)} collective-permute-done((f32[8,1,128]{2,1,0:T(1,128)S(1)}, f32[8,1,128]{2,1,0:T(1,128)S(1)}, u32[]{:S(2)}, u32[]{:S(2)}) %collective-permute-start.37) | collective-permute-done | bytes 4128 | tf_op jit(solution)/shard_map/ppermute | solution.py:36
  224.6 1.1 collective-permute-start.39
  226.5 1.8 collective-permute-done.38
  228.3 1.9 collective-permute-done.39
  (117 shorter events, 25.8 us)
Async XLA Ops:
  86.6 8.2 %collective-permute-start.4 = (f32[4,8,2,160]{3,0,2,1:T(4,128)S(1)}, f32[4,8,2,160]{3,0,2,1:T(4,128)S(1)}, u32[]{:S(2)}, u32[]{:S(2)}) collective-permute-start(f32[4,8,2,160]{3,0,2,1:T(4,128)S(1)} %get-tuple-element.129), channel_id=1, source_target_pairs={{28,0},{0,4},{4,8},{8,12},{12,16},{16,20},{20,24},{24,28},{29,1},{... | collective-permute-start | bytes 122888 | tf_op jit(solution)/shard_map/ppermute | solution.py:26
  87.2 11.8 %collective-permute-start = (f32[8,1,128]{2,1,0:T(1,128)S(1)}, f32[8,1,128]{2,1,0:T(1,128)S(1)}, u32[]{:S(2)}, u32[]{:S(2)}) collective-permute-start(f32[8,1,128]{2,1,0:T(1,128)S(1)} %broadcast.243), channel_id=1, source_target_pairs={{4,0},{8,4},{12,8},{16,12},{20,16},{24,20},{28,24},{0,28},{5,1},{9... | collective-permute-start | bytes 12296 | tf_op jit(solution)/shard_map/ppermute | solution.py:38
  91.3 7.7 %collective-permute-start.1 = (f32[8,1,128]{2,1,0:T(1,128)S(1)}, f32[8,1,128]{2,1,0:T(1,128)S(1)}, u32[]{:S(2)}, u32[]{:S(2)}) collective-permute-start(f32[8,1,128]{2,1,0:T(1,128)S(1)} %broadcast.243), channel_id=1, source_target_pairs={{0,4},{4,8},{8,12},{12,16},{16,20},{20,24},{24,28},{28,0},{1,5},{5... | collective-permute-start | bytes 12296 | tf_op jit(solution)/shard_map/ppermute | solution.py:36
  91.3 5.4 %collective-permute-start.5 = (f32[4,8,2,160]{3,0,2,1:T(4,128)S(1)}, f32[4,8,2,160]{3,0,2,1:T(4,128)S(1)}, u32[]{:S(2)}, u32[]{:S(2)}) collective-permute-start(f32[4,8,2,160]{3,0,2,1:T(4,128)S(1)} %get-tuple-element.128), channel_id=1, source_target_pairs={{4,0},{8,4},{12,8},{16,12},{20,16},{24,20},{28,24},{0,28},{5,1},{9... | collective-permute-start | bytes 122888 | tf_op jit(solution)/shard_map/ppermute | solution.py:26
  96.9 10.2 %collective-permute-start.6 = (f32[4,8,16,16]{3,0,2,1:T(4,128)S(1)}, f32[4,8,16,16]{3,0,2,1:T(4,128)S(1)}, u32[]{:S(2)}, u32[]{:S(2)}) collective-permute-start(f32[4,8,16,16]{3,0,2,1:T(4,128)S(1)} %get-tuple-element.131), channel_id=1, source_target_pairs={{3,0},{0,1},{1,2},{2,3},{7,4},{4,5},{5,6},{6,7},{11,8},{8,9},{9,10... | collective-permute-start | bytes 98312 | tf_op jit(solution)/shard_map/ppermute | solution.py:26
  99.2 12.2 %collective-permute-start.7 = (f32[4,8,16,16]{3,0,2,1:T(4,128)S(1)}, f32[4,8,16,16]{3,0,2,1:T(4,128)S(1)}, u32[]{:S(2)}, u32[]{:S(2)}) collective-permute-start(f32[4,8,16,16]{3,0,2,1:T(4,128)S(1)} %get-tuple-element.130), channel_id=1, source_target_pairs={{1,0},{2,1},{3,2},{0,3},{5,4},{6,5},{7,6},{4,7},{9,8},{10,9},{11,1... | collective-permute-start | bytes 98312 | tf_op jit(solution)/shard_map/ppermute | solution.py:26
  132.8 4.8 %collective-permute-start.8 = (f32[8,1,128]{2,1,0:T(1,128)S(1)}, f32[8,1,128]{2,1,0:T(1,128)S(1)}, u32[]{:S(2)}, u32[]{:S(2)}) collective-permute-start(f32[8,1,128]{2,1,0:T(1,128)S(1)} %get-tuple-element.165), channel_id=1, source_target_pairs={{4,0},{8,4},{12,8},{16,12},{20,16},{24,20},{28,24},{0,28},{5,1},{9... | collective-permute-start | bytes 12296 | tf_op jit(solution)/shard_map/ppermute | solution.py:38
  135.4 4.8 %collective-permute-start.9 = (f32[8,1,128]{2,1,0:T(1,128)S(1)}, f32[8,1,128]{2,1,0:T(1,128)S(1)}, u32[]{:S(2)}, u32[]{:S(2)}) collective-permute-start(f32[8,1,128]{2,1,0:T(1,128)S(1)} %get-tuple-element.164), channel_id=1, source_target_pairs={{0,4},{4,8},{8,12},{12,16},{16,20},{20,24},{24,28},{28,0},{1,5},{5... | collective-permute-start | bytes 12296 | tf_op jit(solution)/shard_map/ppermute | solution.py:36
  135.5 6.9 %collective-permute-start.2 = (f32[8,18,1]{2,1,0:T(8,128)S(1)}, f32[8,18,1]{2,1,0:T(8,128)S(1)}, u32[]{:S(2)}, u32[]{:S(2)}) collective-permute-start(f32[8,18,1]{2,1,0:T(8,128)S(1)} %get-tuple-element.148), channel_id=1, source_target_pairs={{1,0},{2,1},{3,2},{0,3},{5,4},{6,5},{7,6},{4,7},{9,8},{10,9},{11,1... | collective-permute-start | bytes 1736 | tf_op jit(solution)/shard_map/ppermute | solution.py:38
  137.1 7.0 %collective-permute-start.3 = (f32[8,18,1]{2,1,0:T(8,128)S(1)}, f32[8,18,1]{2,1,0:T(8,128)S(1)}, u32[]{:S(2)}, u32[]{:S(2)}) collective-permute-start(f32[8,18,1]{2,1,0:T(8,128)S(1)} %get-tuple-element.149), channel_id=1, source_target_pairs={{0,1},{1,2},{2,3},{3,0},{4,5},{5,6},{6,7},{7,4},{8,9},{9,10},{10,1... | collective-permute-start | bytes 1736 | tf_op jit(solution)/shard_map/ppermute | solution.py:36
  140.4 4.7 %collective-permute-start.10 = (f32[8,18,1]{2,1,0:T(8,128)S(1)}, f32[8,18,1]{2,1,0:T(8,128)S(1)}, u32[]{:S(2)}, u32[]{:S(2)}) collective-permute-start(f32[8,18,1]{2,1,0:T(8,128)S(1)} %get-tuple-element.146), channel_id=1, source_target_pairs={{1,0},{2,1},{3,2},{0,3},{5,4},{6,5},{7,6},{4,7},{9,8},{10,9},{11,1... | collective-permute-start | bytes 1736 | tf_op jit(solution)/shard_map/ppermute | solution.py:38
  142.0 5.5 %collective-permute-start.11 = (f32[8,18,1]{2,1,0:T(8,128)S(1)}, f32[8,18,1]{2,1,0:T(8,128)S(1)}, u32[]{:S(2)}, u32[]{:S(2)}) collective-permute-start(f32[8,18,1]{2,1,0:T(8,128)S(1)} %get-tuple-element.147), channel_id=1, source_target_pairs={{0,1},{1,2},{2,3},{3,0},{4,5},{5,6},{6,7},{7,4},{8,9},{9,10},{10,1... | collective-permute-start | bytes 1736 | tf_op jit(solution)/shard_map/ppermute | solution.py:36
  147.7 2.7 %collective-permute-start.12 = (f32[8,1,128]{2,1,0:T(1,128)S(1)}, f32[8,1,128]{2,1,0:T(1,128)S(1)}, u32[]{:S(2)}, u32[]{:S(2)}) collective-permute-start(f32[8,1,128]{2,1,0:T(1,128)S(1)} %get-tuple-element.163), channel_id=1, source_target_pairs={{4,0},{8,4},{12,8},{16,12},{20,16},{24,20},{28,24},{0,28},{5,1},{9... | collective-permute-start | bytes 12296 | tf_op jit(solution)/shard_map/ppermute | solution.py:38
  149.1 4.8 %collective-permute-start.13 = (f32[8,1,128]{2,1,0:T(1,128)S(1)}, f32[8,1,128]{2,1,0:T(1,128)S(1)}, u32[]{:S(2)}, u32[]{:S(2)}) collective-permute-start(f32[8,1,128]{2,1,0:T(1,128)S(1)} %get-tuple-element.162), channel_id=1, source_target_pairs={{0,4},{4,8},{8,12},{12,16},{16,20},{20,24},{24,28},{28,0},{1,5},{5... | collective-permute-start | bytes 12296 | tf_op jit(solution)/shard_map/ppermute | solution.py:36
  154.1 4.7 %collective-permute-start.14 = (f32[8,18,1]{2,1,0:T(8,128)S(1)}, f32[8,18,1]{2,1,0:T(8,128)S(1)}, u32[]{:S(2)}, u32[]{:S(2)}) collective-permute-start(f32[8,18,1]{2,1,0:T(8,128)S(1)} %get-tuple-element.144), channel_id=1, source_target_pairs={{1,0},{2,1},{3,2},{0,3},{5,4},{6,5},{7,6},{4,7},{9,8},{10,9},{11,1... | collective-permute-start | bytes 1736 | tf_op jit(solution)/shard_map/ppermute | solution.py:38
  154.9 5.5 %collective-permute-start.15 = (f32[8,18,1]{2,1,0:T(8,128)S(1)}, f32[8,18,1]{2,1,0:T(8,128)S(1)}, u32[]{:S(2)}, u32[]{:S(2)}) collective-permute-start(f32[8,18,1]{2,1,0:T(8,128)S(1)} %get-tuple-element.145), channel_id=1, source_target_pairs={{0,1},{1,2},{2,3},{3,0},{4,5},{5,6},{6,7},{7,4},{8,9},{9,10},{10,1... | collective-permute-start | bytes 1736 | tf_op jit(solution)/shard_map/ppermute | solution.py:36
  160.6 1.4 collective-permute-start.16
  160.7 4.9 %collective-permute-start.17 = (f32[8,1,128]{2,1,0:T(1,128)S(1)}, f32[8,1,128]{2,1,0:T(1,128)S(1)}, u32[]{:S(2)}, u32[]{:S(2)}) collective-permute-start(f32[8,1,128]{2,1,0:T(1,128)S(1)} %get-tuple-element.160), channel_id=1, source_target_pairs={{0,4},{4,8},{8,12},{12,16},{16,20},{20,24},{24,28},{28,0},{1,5},{5... | collective-permute-start | bytes 12296 | tf_op jit(solution)/shard_map/ppermute | solution.py:36
  165.7 4.7 %collective-permute-start.18 = (f32[8,18,1]{2,1,0:T(8,128)S(1)}, f32[8,18,1]{2,1,0:T(8,128)S(1)}, u32[]{:S(2)}, u32[]{:S(2)}) collective-permute-start(f32[8,18,1]{2,1,0:T(8,128)S(1)} %get-tuple-element.142), channel_id=1, source_target_pairs={{1,0},{2,1},{3,2},{0,3},{5,4},{6,5},{7,6},{4,7},{9,8},{10,9},{11,1... | collective-permute-start | bytes 1736 | tf_op jit(solution)/shard_map/ppermute | solution.py:38
  166.5 5.5 %collective-permute-start.19 = (f32[8,18,1]{2,1,0:T(8,128)S(1)}, f32[8,18,1]{2,1,0:T(8,128)S(1)}, u32[]{:S(2)}, u32[]{:S(2)}) collective-permute-start(f32[8,18,1]{2,1,0:T(8,128)S(1)} %get-tuple-element.143), channel_id=1, source_target_pairs={{0,1},{1,2},{2,3},{3,0},{4,5},{5,6},{6,7},{7,4},{8,9},{9,10},{10,1... | collective-permute-start | bytes 1736 | tf_op jit(solution)/shard_map/ppermute | solution.py:36
  172.2 1.4 collective-permute-start.20
  172.3 4.9 %collective-permute-start.21 = (f32[8,1,128]{2,1,0:T(1,128)S(1)}, f32[8,1,128]{2,1,0:T(1,128)S(1)}, u32[]{:S(2)}, u32[]{:S(2)}) collective-permute-start(f32[8,1,128]{2,1,0:T(1,128)S(1)} %get-tuple-element.158), channel_id=1, source_target_pairs={{0,4},{4,8},{8,12},{12,16},{16,20},{20,24},{24,28},{28,0},{1,5},{5... | collective-permute-start | bytes 12296 | tf_op jit(solution)/shard_map/ppermute | solution.py:36
  177.3 4.7 %collective-permute-start.22 = (f32[8,18,1]{2,1,0:T(8,128)S(1)}, f32[8,18,1]{2,1,0:T(8,128)S(1)}, u32[]{:S(2)}, u32[]{:S(2)}) collective-permute-start(f32[8,18,1]{2,1,0:T(8,128)S(1)} %get-tuple-element.140), channel_id=1, source_target_pairs={{1,0},{2,1},{3,2},{0,3},{5,4},{6,5},{7,6},{4,7},{9,8},{10,9},{11,1... | collective-permute-start | bytes 1736 | tf_op jit(solution)/shard_map/ppermute | solution.py:38
  178.3 5.5 %collective-permute-start.23 = (f32[8,18,1]{2,1,0:T(8,128)S(1)}, f32[8,18,1]{2,1,0:T(8,128)S(1)}, u32[]{:S(2)}, u32[]{:S(2)}) collective-permute-start(f32[8,18,1]{2,1,0:T(8,128)S(1)} %get-tuple-element.141), channel_id=1, source_target_pairs={{0,1},{1,2},{2,3},{3,0},{4,5},{5,6},{6,7},{7,4},{8,9},{9,10},{10,1... | collective-permute-start | bytes 1736 | tf_op jit(solution)/shard_map/ppermute | solution.py:36
  184.0 1.4 collective-permute-start.24
  184.0 4.9 %collective-permute-start.25 = (f32[8,1,128]{2,1,0:T(1,128)S(1)}, f32[8,1,128]{2,1,0:T(1,128)S(1)}, u32[]{:S(2)}, u32[]{:S(2)}) collective-permute-start(f32[8,1,128]{2,1,0:T(1,128)S(1)} %get-tuple-element.156), channel_id=1, source_target_pairs={{0,4},{4,8},{8,12},{12,16},{16,20},{20,24},{24,28},{28,0},{1,5},{5... | collective-permute-start | bytes 12296 | tf_op jit(solution)/shard_map/ppermute | solution.py:36
  189.0 4.7 %collective-permute-start.26 = (f32[8,18,1]{2,1,0:T(8,128)S(1)}, f32[8,18,1]{2,1,0:T(8,128)S(1)}, u32[]{:S(2)}, u32[]{:S(2)}) collective-permute-start(f32[8,18,1]{2,1,0:T(8,128)S(1)} %get-tuple-element.138), channel_id=1, source_target_pairs={{1,0},{2,1},{3,2},{0,3},{5,4},{6,5},{7,6},{4,7},{9,8},{10,9},{11,1... | collective-permute-start | bytes 1736 | tf_op jit(solution)/shard_map/ppermute | solution.py:38
  189.7 5.5 %collective-permute-start.27 = (f32[8,18,1]{2,1,0:T(8,128)S(1)}, f32[8,18,1]{2,1,0:T(8,128)S(1)}, u32[]{:S(2)}, u32[]{:S(2)}) collective-permute-start(f32[8,18,1]{2,1,0:T(8,128)S(1)} %get-tuple-element.139), channel_id=1, source_target_pairs={{0,1},{1,2},{2,3},{3,0},{4,5},{5,6},{6,7},{7,4},{8,9},{9,10},{10,1... | collective-permute-start | bytes 1736 | tf_op jit(solution)/shard_map/ppermute | solution.py:36
  195.4 1.4 collective-permute-start.28
  195.4 4.9 %collective-permute-start.29 = (f32[8,1,128]{2,1,0:T(1,128)S(1)}, f32[8,1,128]{2,1,0:T(1,128)S(1)}, u32[]{:S(2)}, u32[]{:S(2)}) collective-permute-start(f32[8,1,128]{2,1,0:T(1,128)S(1)} %get-tuple-element.154), channel_id=1, source_target_pairs={{0,4},{4,8},{8,12},{12,16},{16,20},{20,24},{24,28},{28,0},{1,5},{5... | collective-permute-start | bytes 12296 | tf_op jit(solution)/shard_map/ppermute | solution.py:36
  200.4 4.7 %collective-permute-start.30 = (f32[8,18,1]{2,1,0:T(8,128)S(1)}, f32[8,18,1]{2,1,0:T(8,128)S(1)}, u32[]{:S(2)}, u32[]{:S(2)}) collective-permute-start(f32[8,18,1]{2,1,0:T(8,128)S(1)} %get-tuple-element.136), channel_id=1, source_target_pairs={{1,0},{2,1},{3,2},{0,3},{5,4},{6,5},{7,6},{4,7},{9,8},{10,9},{11,1... | collective-permute-start | bytes 1736 | tf_op jit(solution)/shard_map/ppermute | solution.py:38
  201.3 5.5 %collective-permute-start.31 = (f32[8,18,1]{2,1,0:T(8,128)S(1)}, f32[8,18,1]{2,1,0:T(8,128)S(1)}, u32[]{:S(2)}, u32[]{:S(2)}) collective-permute-start(f32[8,18,1]{2,1,0:T(8,128)S(1)} %get-tuple-element.137), channel_id=1, source_target_pairs={{0,1},{1,2},{2,3},{3,0},{4,5},{5,6},{6,7},{7,4},{8,9},{9,10},{10,1... | collective-permute-start | bytes 1736 | tf_op jit(solution)/shard_map/ppermute | solution.py:36
  206.9 1.4 collective-permute-start.32
  207.0 4.9 %collective-permute-start.33 = (f32[8,1,128]{2,1,0:T(1,128)S(1)}, f32[8,1,128]{2,1,0:T(1,128)S(1)}, u32[]{:S(2)}, u32[]{:S(2)}) collective-permute-start(f32[8,1,128]{2,1,0:T(1,128)S(1)} %get-tuple-element.152), channel_id=1, source_target_pairs={{0,4},{4,8},{8,12},{12,16},{16,20},{20,24},{24,28},{28,0},{1,5},{5... | collective-permute-start | bytes 12296 | tf_op jit(solution)/shard_map/ppermute | solution.py:36
  212.0 4.7 %collective-permute-start.34 = (f32[8,18,1]{2,1,0:T(8,128)S(1)}, f32[8,18,1]{2,1,0:T(8,128)S(1)}, u32[]{:S(2)}, u32[]{:S(2)}) collective-permute-start(f32[8,18,1]{2,1,0:T(8,128)S(1)} %get-tuple-element.134), channel_id=1, source_target_pairs={{1,0},{2,1},{3,2},{0,3},{5,4},{6,5},{7,6},{4,7},{9,8},{10,9},{11,1... | collective-permute-start | bytes 1736 | tf_op jit(solution)/shard_map/ppermute | solution.py:38
  212.9 5.5 %collective-permute-start.35 = (f32[8,18,1]{2,1,0:T(8,128)S(1)}, f32[8,18,1]{2,1,0:T(8,128)S(1)}, u32[]{:S(2)}, u32[]{:S(2)}) collective-permute-start(f32[8,18,1]{2,1,0:T(8,128)S(1)} %get-tuple-element.135), channel_id=1, source_target_pairs={{0,1},{1,2},{2,3},{3,0},{4,5},{5,6},{6,7},{7,4},{8,9},{9,10},{10,1... | collective-permute-start | bytes 1736 | tf_op jit(solution)/shard_map/ppermute | solution.py:36
  218.6 1.4 collective-permute-start.36
  218.6 4.9 %collective-permute-start.37 = (f32[8,1,128]{2,1,0:T(1,128)S(1)}, f32[8,1,128]{2,1,0:T(1,128)S(1)}, u32[]{:S(2)}, u32[]{:S(2)}) collective-permute-start(f32[8,1,128]{2,1,0:T(1,128)S(1)} %get-tuple-element.150), channel_id=1, source_target_pairs={{0,4},{4,8},{8,12},{12,16},{16,20},{20,24},{24,28},{28,0},{1,5},{5... | collective-permute-start | bytes 12296 | tf_op jit(solution)/shard_map/ppermute | solution.py:36
  223.6 4.7 %collective-permute-start.38 = (f32[8,18,1]{2,1,0:T(8,128)S(1)}, f32[8,18,1]{2,1,0:T(8,128)S(1)}, u32[]{:S(2)}, u32[]{:S(2)}) collective-permute-start(f32[8,18,1]{2,1,0:T(8,128)S(1)} %get-tuple-element.132), channel_id=1, source_target_pairs={{1,0},{2,1},{3,2},{0,3},{5,4},{6,5},{7,6},{4,7},{9,8},{10,9},{11,1... | collective-permute-start | bytes 1736 | tf_op jit(solution)/shard_map/ppermute | solution.py:38
  224.6 5.5 %collective-permute-start.39 = (f32[8,18,1]{2,1,0:T(8,128)S(1)}, f32[8,18,1]{2,1,0:T(8,128)S(1)}, u32[]{:S(2)}, u32[]{:S(2)}) collective-permute-start(f32[8,18,1]{2,1,0:T(8,128)S(1)} %get-tuple-element.133), channel_id=1, source_target_pairs={{0,1},{1,2},{2,3},{3,0},{4,5},{5,6},{6,7},{7,4},{8,9},{9,10},{10,1... | collective-permute-start | bytes 1736 | tf_op jit(solution)/shard_map/ppermute | solution.py:36
where the time goes:
time: 232 us; the launch traced here: 231 us
  waiting for transfers between devices  77 us (33%)
  matrix products  49.4 us (21%)
  starting transfers between devices  37.3 us (16%)
  other arithmetic  36.2 us (16%)
  local copies, waits for them, and re-layouts  29.6 us (13%)
    dot_general x8, matrix products, add_block(): lax.dot_general(left_hot, right_hot, (((0,), (0,)), ((), ())), precision=...  49.4 us
    ppermute x18, waiting for transfers between devices, extended_2(): lax.ppermute(tail, axis, [(i, (i + 1) % count) for i in range(count)])  43.6 us
    scatter-add x2, local copies, waits for them, and re-layouts, shards(): interior.at[:, :, :, :MY].add(from_below).at[:, :, :, CY - MY:]  25.1 us
    ppermute x18, waiting for transfers between devices, extended_2(): lax.ppermute(head, axis, [((i + 1) % count, i) for i in range(count)])  24.6 us
    mul x8, other arithmetic, add_block(): (col_part[:, None, None] == col_ids).astype(jnp.float32)  23.8 us
    ppermute x18, starting transfers between devices, extended_2(): lax.ppermute(head, axis, [((i + 1) % count, i) for i in range(count)])  17.8 us
    ppermute x18, starting transfers between devices, extended_2(): lax.ppermute(tail, axis, [(i, (i + 1) % count) for i in range(count)])  12.4 us
    ppermute x4, waiting for transfers between devices, from_behind(): return lax.ppermute(block, axis, route)  8.75 us
  transfers between devices with their start and end apart: 40, of which 34 were waited for; matrix products, arithmetic and copies ran while one was open for 2% of the time, Pallas kernels for 0%

commit v1 on v0

v1 whole, which is shorter than its diff:
```python
import functools

import jax
import jax.numpy as jnp
from jax import lax
from jax.experimental import pallas as pl
from jax.experimental.pallas import tpu as pltpu
from jax.sharding import PartitionSpec as P

CX = 16
CY = 128
NZ = 8
SWEEPS = 4
MX = 2
MY = 16
HALO = 8
BLOCK = 1024
STAY = 64
LEAVE = 48

SCREENING = 0.5
CUBIC_TERM = 0.3
COUPLING = 1.5
SMOOTHING = 0.1
BACKGROUND = 1.0

MESH = pl.DeviceIdType.MESH
STEPS = ((1, 0), (-1, 0), (0, 1), (0, -1), (1, 1), (1, -1), (-1, 1), (-1, -1))


def deposit_kernel(counts, payload, cells, main, xs, ys, cs, stay_acc, leave_acc):
    part = payload.shape[1]
    limits = []
    total = jnp.int32(0)
    for e in range(8):
        total = total + counts[0, e]
        limits.append(total)
    stay_acc[...] = jnp.zeros_like(stay_acc)
    leave_acc[...] = jnp.zeros_like(leave_acc)

    def hot_rows(count, index):
        ids = lax.broadcasted_iota(jnp.int32, (count, BLOCK), 0)
        return jnp.where(ids == index, 1.0, 0.0).astype(jnp.bfloat16)

    def step(b, carry):
        start = pl.multiple_of(b * BLOCK, BLOCK)
        span = pl.ds(start, BLOCK)
        position = start + lax.broadcasted_iota(jnp.int32, (1, BLOCK), 1)
        direction = jnp.zeros((1, BLOCK), jnp.int32)
        for e in range(8):
            direction = direction + (position >= limits[e]).astype(jnp.int32)
        k = cells[0:1, span]
        i = cells[1:2, span]
        j = cells[2:3, span]
        stays = direction == 8
        chunk = k * MY + (j & (MY - 1))
        layer = i & 1
        leave_row = jnp.where(
            direction < 2, k * MX + layer, jnp.where(direction < 4, 16 + i, 28 + direction)
        )
        leave_col = jnp.where(
            direction < 2,
            direction * CY + j,
            jnp.where(direction < 4, (direction - 2) * CY, layer * CY) + chunk,
        )
        stay_row = jnp.where(stays, k * 8 + (i & 7), -1)
        leave_row = jnp.where(stays, -1, leave_row)
        col = jnp.where(stays, (i >> 3) * CY + j, leave_col)
        cols_hot = hot_rows(2 * CY, col)
        mass = payload[0:1, span]
        values = [mass] + [mass * payload[c : c + 1, span] for c in range(1, 4)]
        highs = [v.astype(jnp.bfloat16).astype(jnp.float32) for v in values]
        lows = [v - h for v, h in zip(values, highs)]
        wide = [jnp.broadcast_to(v, (16, BLOCK)).astype(jnp.bfloat16) for v in highs + lows]

        def add(acc, count, index):
            hot = hot_rows(count, index).reshape(count // 16, 16, BLOCK)
            left = jnp.concatenate(
                [(hot * w[None]).reshape(count, BLOCK) for w in wide], axis=0
            )
            acc[...] += lax.dot_general(
                left, cols_hot, (((1,), (1,)), ((), ())), preferred_element_type=jnp.float32
            )

        @pl.when(start + BLOCK > limits[7])
        def _():
            add(stay_acc, STAY, stay_row)

        @pl.when(start < limits[7])
        def _():
            add(leave_acc, LEAVE, leave_row)

        return carry

    lax.fori_loop(0, part // BLOCK, step, 0)
    for c in range(4):
        for h in range(2):
            lanes = slice(h * CY, (h + 1) * CY)
            whole = (
                stay_acc[c * STAY : (c + 1) * STAY, lanes]
                + stay_acc[(4 + c) * STAY : (5 + c) * STAY, lanes]
            )
            main[c, :, 8 * h : 8 * h + 8, :] = whole.reshape(NZ, 8, CY)
            out = (
                leave_acc[c * LEAVE : (c + 1) * LEAVE, lanes]
                + leave_acc[(4 + c) * LEAVE : (5 + c) * LEAVE, lanes]
            )
            xs[h, c] = out[0:16]
            ys[h, c] = out[16:32]
            for d in range(4):
                cs[d, 2 * c + h : 2 * c + h + 1, :] = out[32 + d : 33 + d]


def relax_kernel(
    sizes, main, xs, ys, cs, field, momentum,
    rx, ry, rc, dens, edges, hx, hy, ext, src, u,
    send1, recv1, send2, recv2,
):
    n_gx, n_gy = sizes
    me_x = lax.axis_index("gx")
    me_y = lax.axis_index("gy")

    def device(step):
        return (lax.rem(me_x + step[0] + n_gx, n_gx), lax.rem(me_y + step[1] + n_gy, n_gy))

    barrier = pltpu.get_barrier_semaphore()
    for step in STEPS:
        pl.semaphore_signal(barrier, inc=1, device_id=device(step), device_id_type=MESH)
    pl.semaphore_wait(barrier, 8)

    def remote(src_ref, dst_ref, sems, recvs, d):
        return pltpu.make_async_remote_copy(
            src_ref=src_ref, dst_ref=dst_ref, send_sem=sems.at[d], recv_sem=recvs.at[d],
            device_id=device(STEPS[d]), device_id_type=MESH,
        )

    first = []
    for d in range(8):
        if d < 2:
            pair = (xs.at[d], rx.at[d])
        elif d < 4:
            pair = (ys.at[d - 2], ry.at[d - 2])
        else:
            pair = (cs.at[d - 4], rc.at[d - 4])
        first.append(remote(pair[0], pair[1], send1, recv1, d))
    for copy in first:
        copy.start()
    lane = lax.broadcasted_iota(jnp.int32, (1, CY), 1)
    lane16 = lax.broadcasted_iota(jnp.int32, (CX, CY), 1)
    for copy in first:
        copy.wait_recv()

    def collected(c):
        sides = []
        for s in range(2):
            low = rc[s, 2 * c : 2 * c + 2, :]
            high = rc[2 + s, 2 * c : 2 * c + 2, :]
            pad = jnp.zeros((CX - 2 * MX, CY), jnp.float32)
            sides.append(ry[s, c] + jnp.concatenate([low, pad, high], axis=0))
        pad = jnp.zeros((CX - 2 * MX, CY), jnp.float32)
        out = []
        for k in range(NZ):
            left = pltpu.roll(sides[0], (CY - MY * k) % CY, axis=1)
            right = pltpu.roll(sides[1], (2 * CY - MY - MY * k) % CY, axis=1)
            extra = jnp.where(lane16 < MY, left, jnp.where(lane16 >= CY - MY, right, 0.0))
            faces = jnp.concatenate(
                [rx[0, c, 2 * k : 2 * k + 2, :], pad, rx[1, c, 2 * k : 2 * k + 2, :]], axis=0
            )
            out.append(main[c, k] + faces + extra)
        return out

    rho = collected(0)
    low_edge = jnp.zeros((CX, CY), jnp.float32)
    high_edge = jnp.zeros((CX, CY), jnp.float32)
    for k in range(NZ):
        dens[k] = rho[k]
        here = (lane16 >= MY * k) & (lane16 < MY * (k + 1))
        low_edge = jnp.where(here, pltpu.roll(rho[k], MY * k, axis=1), low_edge)
        high_edge = jnp.where(here, pltpu.roll(rho[k], (MY * (k + 1)) % CY, axis=1), high_edge)
    edges[0] = low_edge
    edges[1] = high_edge

    second = [
        (dens.at[:, 8:16, :], hx.at[0]),
        (dens.at[:, 0:8, :], hx.at[1]),
        (edges.at[1], hy.at[1, 8:24, :]),
        (edges.at[0], hy.at[0, 8:24, :]),
        (edges.at[1, 8:16, :], hy.at[1, 0:8, :]),
        (edges.at[0, 8:16, :], hy.at[0, 0:8, :]),
        (edges.at[1, 0:8, :], hy.at[1, 24:32, :]),
        (edges.at[0, 0:8, :], hy.at[0, 24:32, :]),
    ]
    second = [remote(a, b, send2, recv2, d) for d, (a, b) in enumerate(second)]
    for copy in second:
        copy.start()
    for c in range(1, 4):
        for k, layer in enumerate(collected(c)):
            momentum[c - 1, k] = layer
    for copy in second:
        copy.wait_recv()

    lane32 = lax.broadcasted_iota(jnp.int32, (32, CY), 1)
    for k in range(NZ):
        ext[k, 0:8, 0:CY] = hx[0, k]
        ext[k, 8:24, 0:CY] = dens[k]
        ext[k, 24:32, 0:CY] = hx[1, k]
        after = pltpu.roll(hy[0], (CY - MY * k) % CY, axis=1)
        before = pltpu.roll(hy[1], (2 * CY - MY - MY * k) % CY, axis=1)
        ext[k, :, CY:] = jnp.where(
            lane32 < MY, after, jnp.where(lane32 >= CY - MY, before, 0.0)
        )

    def around(ref, k):
        mid = ref[k]
        total = (
            pltpu.roll(mid, 1, axis=0)
            + pltpu.roll(mid, 31, axis=0)
            + pltpu.roll(mid, 1, axis=1)
            + pltpu.roll(mid, 2 * CY - 1, axis=1)
        )
        if k > 0:
            total = total + ref[k - 1]
        if k < NZ - 1:
            total = total + ref[k + 1]
        return mid, total

    odd = (
        lax.broadcasted_iota(jnp.int32, (32, 2 * CY), 0)
        + lax.broadcasted_iota(jnp.int32, (32, 2 * CY), 1)
    ) & 1
    for k in range(NZ):
        mid, near = around(ext, k)
        value = COUPLING * (mid + SMOOTHING * (near - 6.0 * mid) - BACKGROUND)
        src[k] = value
        u[k] = jnp.where(odd == (k & 1), value * (-1.0 / (6.0 + SCREENING)), 0.0)

    def half(colour):
        for k in range(NZ):
            mid, near = around(u, k)
            square = mid * mid
            r = near - (6.0 + SCREENING) * mid - CUBIC_TERM * square * mid - src[k]
            s = -(6.0 + SCREENING) - (3.0 * CUBIC_TERM) * square
            u[k] = jnp.where(odd == ((k + colour) & 1), mid - r / s, mid)

    half(1)

    def sweep(n, carry):
        half(0)
        half(1)
        return carry

    lax.fori_loop(0, SWEEPS - 1, sweep, 0)
    for k in range(NZ):
        field[k] = u[k, 8:24, 0:CY]
    for copy in first + second:
        copy.wait_send()


def shards(sizes, payload, cells, counts):
    f32 = jnp.float32
    vmem = pl.BlockSpec(memory_space=pltpu.VMEM)
    smem = pl.BlockSpec(memory_space=pltpu.SMEM)
    main, xs, ys, cs = pl.pallas_call(
        deposit_kernel,
        out_shape=(
            jax.ShapeDtypeStruct((4, NZ, CX, CY), f32),
            jax.ShapeDtypeStruct((2, 4, NZ * MX, CY), f32),
            jax.ShapeDtypeStruct((2, 4, CX, CY), f32),
            jax.ShapeDtypeStruct((4, 8, CY), f32),
        ),
        in_specs=[smem, vmem, vmem],
        out_specs=(vmem,) * 4,
        scratch_shapes=[
            pltpu.VMEM((8 * STAY, 2 * CY), f32),
            pltpu.VMEM((8 * LEAVE, 2 * CY), f32),
        ],
        compiler_params=pltpu.CompilerParams(vmem_limit_bytes=40 * 1024 * 1024),
        name="deposit",
    )(counts, payload, cells)
    field, momentum = pl.pallas_call(
        functools.partial(relax_kernel, sizes),
        out_shape=(
            jax.ShapeDtypeStruct((NZ, CX, CY), f32),
            jax.ShapeDtypeStruct((3, NZ, CX, CY), f32),
        ),
        in_specs=[vmem] * 4,
        out_specs=(vmem,) * 2,
        scratch_shapes=[
            pltpu.VMEM((2, 4, NZ * MX, CY), f32),
            pltpu.VMEM((2, 4, CX, CY), f32),
            pltpu.VMEM((4, 8, CY), f32),
            pltpu.VMEM((NZ, CX, CY), f32),
            pltpu.VMEM((2, CX, CY), f32),
            pltpu.VMEM((2, NZ, 8, CY), f32),
            pltpu.VMEM((2, 32, CY), f32),
            pltpu.VMEM((NZ, 32, 2 * CY), f32),
            pltpu.VMEM((NZ, 32, 2 * CY), f32),
            pltpu.VMEM((NZ, 32, 2 * CY), f32),
        ] + [pltpu.SemaphoreType.DMA((8,))] * 4,
        compiler_params=pltpu.CompilerParams(
            collective_id=0, has_side_effects=True, vmem_limit_bytes=40 * 1024 * 1024
        ),
        name="relax",
    )(main, xs, ys, cs)
    return field, momentum


def solution(mesh):
    sizes = (mesh.shape["gx"], mesh.shape["gy"])
    placed = (P(None, ("gx", "gy")), P(None, ("gx", "gy")), P(("gx", "gy"), None))
    return jax.shard_map(
        functools.partial(shards, sizes),
        mesh=mesh,
        in_specs=placed,
        out_specs=(P(None, "gx", "gy"), P(None, None, "gx", "gy")),
        check_vma=False,
    )
```

time: 232 us -> 34.1 us (0.15)
  waiting for transfers between devices: 77 us -> 0 us
  matrix products: 49.4 us -> 0 us
  starting transfers between devices: 37.3 us -> 0 us
  other arithmetic: 36.2 us -> 0 us
  Pallas kernels: 0 us -> 29.5 us
  local copies, waits for them, and re-layouts: 29.6 us -> 3.86 us
    ppermute x40 -> x0, waiting for transfers between devices: 77 us -> none  [the longest x18 43.6 us: extended_2(): lax.ppermute(tail, axis, [(i, (i + 1) % count) for i in range(count)])]
    dot_general x8 -> x0, matrix products: 49.4 us -> none  [add_block(): lax.dot_general(left_hot, right_hot, (((0,), (0,)), ((), ())), precision=...]
    ppermute x40 -> x0, starting transfers between devices: 37.3 us -> none  [the longest x18 17.8 us: extended_2(): lax.ppermute(head, axis, [((i + 1) % count, i) for i in range(count)])]
    pallas_call x0 -> x2, Pallas kernels: none -> 29.5 us  [the longest x1 17.6 us: shards(): pl.pallas_call(functools.partial(relax_kernel, sizes), out_shape=(jax.Sha...]
    scatter-add x2 -> x0, local copies, waits for them, and re-layouts: 25.1 us -> none  [shards(): interior.at[:, :, :, :MY].add(from_below).at[:, :, :, CY - MY:]]
    mul x9 -> x0, other arithmetic: 24.9 us -> none  [the longest x8 23.8 us: add_block(): (col_part[:, None, None] == col_ids).astype(jnp.float32)]
    add x4 -> x0, other arithmetic: 7.22 us -> none  [the longest x2 6.82 us: shards(): col_index = cells[2] + MY + step_y * CY]
    unnamed x1 -> x8, local copies, waits for them, and re-layouts: 0.69 us -> 3.86 us
  transfers between devices with their start and end apart: 40 -> 0, of which waited for: 34 -> 0; matrix products, arithmetic and copies ran while one was open for 2% -> 0% of each run, Pallas kernels for 0% -> 0%
where the time goes in v1:
time: 34.1 us; the launch traced here: 34 us
  Pallas kernels  29.5 us (87%)
  local copies, waits for them, and re-layouts  3.86 us (11%)
  between operations  0.66 us (2%)
    pallas_call x1, Pallas kernels, shards(): pl.pallas_call(functools.partial(relax_kernel, sizes), out_shape=(jax.Sha...  17.6 us
    pallas_call x1, Pallas kernels, shards(): pl.pallas_call(deposit_kernel, out_shape=(jax.ShapeDtypeStruct((4, NZ, CX...  11.9 us
    unnamed x8, local copies, waits for them, and re-layouts  3.86 us

profile of v1, /device:TPU:0, one launch (start us, length us, event | category | flops | bytes accessed | tf_op | source)
XLA Modules:
  0.0 34.0 jit_solution(218583552822793572)
XLA Ops:
  0.6 0.0 copy-start
  0.6 0.9 %copy-done = f32[4,16384]{1,0:T(4,128)S(1)} copy-done((f32[4,16384]{1,0:T(4,128)S(1)}, f32[4,16384]{1,0:T(4,128)}, u32[]{:S(2)}) %copy-start) | copy-done | bytes 262168
  1.6 0.0 copy-start.1
  1.6 0.9 %copy-done.1 = s32[3,16384]{1,0:T(4,128)S(1)} copy-done((s32[3,16384]{1,0:T(4,128)S(1)}, s32[3,16384]{1,0:T(4,128)}, u32[]{:S(2)}) %copy-start.1) | copy-done | bytes 196632
  2.5 0.0 copy-start.2
  2.5 0.7 %copy-done.2 = s32[1,9]{1,0:T(1,128)S(1)} copy-done((s32[1,9]{1,0:T(1,128)S(1)}, s32[1,9]{1,0:T(1,128)}, u32[]{:S(2)}) %copy-start.2) | copy-done | bytes 60
  3.2 11.9 %deposit.1 = (f32[4,8,16,128]{3,2,1,0:T(8,128)S(1)}, f32[2,4,16,128]{3,2,1,0:T(8,128)S(1)}, f32[2,4,16,128]{3,2,1,0:T(8,128)S(1)}, f32[4,8,128]{2,1,0:T(8,128)S(1)}) custom-call(s32[1,9]{1,0:T(1,128)S(1)} %copy-done.2, f32[4,16384]{1,0:T(4,128)S(1)} %copy-done, s32[3,16384]{1,0:T(4,128)S(1)} %copy-done.1), custom_call_target="tpu_custom_call" | custom-call | tf_op jit(solution)/shard_map/deposit/pallas_call | solution.py:263
  15.1 17.6 %relax.1 = (f32[8,16,128]{2,1,0:T(8,128)S(1)}, f32[3,8,16,128]{3,2,1,0:T(8,128)S(1)}) custom-call(f32[4,8,16,128]{3,2,1,0:T(8,128)S(1)} %get-tuple-element.6.main, f32[2,4,16,128]{3,2,1,0:T(8,128)S(1)} %get-tuple-element.7.xs, f32[2,4,16,128]{3,2,1,0:T(8,128)S(1)} %get-tuple-element.8.ys, f32[4,8,128]{2,1,0:T(8,128)S(1)} %get-tuple-element.9.cs), custom_call_target="tpu_custom_call" | custom-call | tf_op jit(solution)/shard_map/relax/pallas_call | solution.py:280
  32.7 0.6 %copy.7 = f32[8,16,128]{2,1,0:T(8,128)} copy(f32[8,16,128]{2,1,0:T(8,128)S(1)} %get-tuple-element.12) | data formatting | bytes 131072
  33.3 0.7 %copy.8 = f32[3,8,16,128]{3,2,1,0:T(8,128)} copy(f32[3,8,16,128]{3,2,1,0:T(8,128)S(1)} %get-tuple-element.13) | data formatting | bytes 393216
Async XLA Ops:
  0.6 1.0 %copy-start = (f32[4,16384]{1,0:T(4,128)S(1)}, f32[4,16384]{1,0:T(4,128)}, u32[]{:S(2)}) copy-start(f32[4,16384]{1,0:T(4,128)} %payload.1) | copy-start | bytes 786436
  1.6 0.9 %copy-start.1 = (s32[3,16384]{1,0:T(4,128)S(1)}, s32[3,16384]{1,0:T(4,128)}, u32[]{:S(2)}) copy-start(s32[3,16384]{1,0:T(4,128)} %cells.1) | copy-start | bytes 589828
  2.5 0.7 %copy-start.2 = (s32[1,9]{1,0:T(1,128)S(1)}, s32[1,9]{1,0:T(1,128)}, u32[]{:S(2)}) copy-start(s32[1,9]{1,0:T(1,128)} %counts.1) | copy-start | bytes 112

commit v2 on v1

--- a/solution.py
+++ b/solution.py
@@ -28,71 +28,78 @@
 STEPS = ((1, 0), (-1, 0), (0, 1), (0, -1), (1, 1), (1, -1), (-1, 1), (-1, -1))
 
 
-def deposit_kernel(counts, payload, cells, main, xs, ys, cs, stay_acc, leave_acc):
+def deposit_kernel(
+    counts, payload, cells, main, xs, ys, cs, stay_acc, leave_acc
+):
     part = payload.shape[1]
+    stay_acc[...] = jnp.zeros_like(stay_acc)
+    leave_acc[...] = jnp.zeros_like(leave_acc)
+    bf16 = jnp.bfloat16
+    base = lax.broadcasted_iota(jnp.int32, (16, 128), 0)
+    ids = [(base + 16 * g).astype(jnp.float32).astype(bf16) for g in range(16)]
+    ids = [jnp.concatenate([v] * (BLOCK // 128), axis=1) for v in ids]
+    one = jnp.ones((16, BLOCK), bf16)
+    none = jnp.zeros((16, BLOCK), bf16)
     limits = []
     total = jnp.int32(0)
     for e in range(8):
         total = total + counts[0, e]
         limits.append(total)
-    stay_acc[...] = jnp.zeros_like(stay_acc)
-    leave_acc[...] = jnp.zeros_like(leave_acc)
-
-    def hot_rows(count, index):
-        ids = lax.broadcasted_iota(jnp.int32, (count, BLOCK), 0)
-        return jnp.where(ids == index, 1.0, 0.0).astype(jnp.bfloat16)
-
-    def step(b, carry):
+
+    def packed(row):
+        return jnp.broadcast_to(row.astype(jnp.float32), (16, BLOCK)).astype(bf16)
+
+    def add(acc, count, span, row, col):
+        col = packed(col)
+        cols_hot = jnp.concatenate([jnp.where(v == col, one, none) for v in ids], axis=0)
+        block = payload[:, span]
+        first = lax.broadcasted_iota(jnp.int32, (4, BLOCK), 0) == 0
+        values = block[0:1] * jnp.where(first, 1.0, block)
+        high = values.astype(bf16).astype(jnp.float32)
+        low = values - high
+        wide = [packed(v[c : c + 1]) for v in (high, low) for c in range(4)]
+        row = packed(row)
+        masks = [ids[g] == row for g in range(count // 16)]
+        left = jnp.concatenate([jnp.where(m, w, none) for w in wide for m in masks], axis=0)
+        acc[...] += lax.dot_general(
+            left, cols_hot, (((1,), (1,)), ((), ())), preferred_element_type=jnp.float32
+        )
+
+    def block_of(b):
         start = pl.multiple_of(b * BLOCK, BLOCK)
         span = pl.ds(start, BLOCK)
         position = start + lax.broadcasted_iota(jnp.int32, (1, BLOCK), 1)
+        return span, position, cells[0:1, span], cells[1:2, span], cells[2:3, span]
+
+    def stay_step(b, carry):
+        span, position, k, i, j = block_of(b)
+        row = jnp.where(position >= limits[7], k * 8 + (i & 7), 255)
+        add(stay_acc, STAY, span, row, (i >> 3) * CY + j)
+        return carry
+
+    def leave_step(b, carry):
+        span, position, k, i, j = block_of(b)
         direction = jnp.zeros((1, BLOCK), jnp.int32)
         for e in range(8):
             direction = direction + (position >= limits[e]).astype(jnp.int32)
-        k = cells[0:1, span]
-        i = cells[1:2, span]
-        j = cells[2:3, span]
-        stays = direction == 8
         chunk = k * MY + (j & (MY - 1))
         layer = i & 1
-        leave_row = jnp.where(
+        row = jnp.where(
             direction < 2, k * MX + layer, jnp.where(direction < 4, 16 + i, 28 + direction)
         )
-        leave_col = jnp.where(
+        col = jnp.where(
             direction < 2,
             direction * CY + j,
             jnp.where(direction < 4, (direction - 2) * CY, layer * CY) + chunk,
         )
-        stay_row = jnp.where(stays, k * 8 + (i & 7), -1)
-        leave_row = jnp.where(stays, -1, leave_row)
-        col = jnp.where(stays, (i >> 3) * CY + j, leave_col)
-        cols_hot = hot_rows(2 * CY, col)
-        mass = payload[0:1, span]
-        values = [mass] + [mass * payload[c : c + 1, span] for c in range(1, 4)]
-        highs = [v.astype(jnp.bfloat16).astype(jnp.float32) for v in values]
-        lows = [v - h for v, h in zip(values, highs)]
-        wide = [jnp.broadcast_to(v, (16, BLOCK)).astype(jnp.bfloat16) for v in highs + lows]
-
-        def add(acc, count, index):
-            hot = hot_rows(count, index).reshape(count // 16, 16, BLOCK)
-            left = jnp.concatenate(
-                [(hot * w[None]).reshape(count, BLOCK) for w in wide], axis=0
-            )
-            acc[...] += lax.dot_general(
-                left, cols_hot, (((1,), (1,)), ((), ())), preferred_element_type=jnp.float32
-            )
-
-        @pl.when(start + BLOCK > limits[7])
-        def _():
-            add(stay_acc, STAY, stay_row)
-
-        @pl.when(start < limits[7])
-        def _():
-            add(leave_acc, LEAVE, leave_row)
-
+        row = jnp.where(direction == 8, 255, row)
+        add(leave_acc, LEAVE, span, row, col)
         return carry
 
-    lax.fori_loop(0, part // BLOCK, step, 0)
+    blocks = part // BLOCK
+    left_blocks = (limits[7] + (BLOCK - 1)) // BLOCK
+    lax.fori_loop(0, left_blocks, leave_step, 0)
+    lax.fori_loop(limits[7] // BLOCK, blocks, stay_step, 0)
     for c in range(4):
         for h in range(2):
             lanes = slice(h * CY, (h + 1) * CY)
@@ -234,24 +241,42 @@
         src[k] = value
         u[k] = jnp.where(odd == (k & 1), value * (-1.0 / (6.0 + SCREENING)), 0.0)
 
+    def relaxed(mid, near, source):
+        square = mid * mid
+        slope = (6.0 + SCREENING) + (3.0 * CUBIC_TERM) * square
+        r = near - source - mid * ((6.0 + SCREENING) + CUBIC_TERM * square)
+        inverse = pl.reciprocal(slope, approx=True)
+        inverse = inverse * (2.0 - slope * inverse)
+        return mid + r * inverse
+
     def half(colour):
         for k in range(NZ):
             mid, near = around(u, k)
-            square = mid * mid
-            r = near - (6.0 + SCREENING) * mid - CUBIC_TERM * square * mid - src[k]
-            s = -(6.0 + SCREENING) - (3.0 * CUBIC_TERM) * square
-            u[k] = jnp.where(odd == ((k + colour) & 1), mid - r / s, mid)
-
-    half(1)
+            new = relaxed(mid, near, src[k])
+            u[k] = jnp.where(odd == ((k + colour) & 1), new, mid)
 
     def sweep(n, carry):
+        half(1)
         half(0)
-        half(1)
         return carry
 
     lax.fori_loop(0, SWEEPS - 1, sweep, 0)
+    odd_tile = odd[8:24, 0:CY]
     for k in range(NZ):
-        field[k] = u[k, 8:24, 0:CY]
+        wide = u[k, 8:24, :]
+        mid = wide[:, 0:CY]
+        near = (
+            u[k, 7:23, 0:CY]
+            + u[k, 9:25, 0:CY]
+            + pltpu.roll(wide, 1, axis=1)[:, 0:CY]
+            + pltpu.roll(wide, 2 * CY - 1, axis=1)[:, 0:CY]
+        )
+        if k > 0:
+            near = near + u[k - 1, 8:24, 0:CY]
+        if k < NZ - 1:
+            near = near + u[k + 1, 8:24, 0:CY]
+        new = relaxed(mid, near, src[k, 8:24, 0:CY])
+        field[k] = jnp.where(odd_tile == ((k + 1) & 1), new, mid)
     for copy in first + second:
         copy.wait_send()
 
@@ -259,7 +284,6 @@
 def shards(sizes, payload, cells, counts):
     f32 = jnp.float32
     vmem = pl.BlockSpec(memory_space=pltpu.VMEM)
-    smem = pl.BlockSpec(memory_space=pltpu.SMEM)
     main, xs, ys, cs = pl.pallas_call(
         deposit_kernel,
         out_shape=(
@@ -268,7 +292,7 @@
             jax.ShapeDtypeStruct((2, 4, CX, CY), f32),
             jax.ShapeDtypeStruct((4, 8, CY), f32),
         ),
-        in_specs=[smem, vmem, vmem],
+        in_specs=[pl.BlockSpec(memory_space=pltpu.SMEM), vmem, vmem],
         out_specs=(vmem,) * 4,
         scratch_shapes=[
             pltpu.VMEM((8 * STAY, 2 * CY), f32),

time: 34.1 us -> 30.7 us (0.900)
  Pallas kernels: 29.5 us -> 26 us
    pallas_call x1, Pallas kernels: 11.9 us -> 8.43 us  [shards(): pl.pallas_call(deposit_kernel, out_shape=(jax.ShapeDtypeStruct((4, NZ, CX...]
where the time goes in v2:
time: 30.7 us; the launch traced here: 30.5 us
  Pallas kernels  26 us (85%)
  local copies, waits for them, and re-layouts  3.86 us (13%)
  between operations  0.66 us (2%)
    pallas_call x1, Pallas kernels, shards(): pl.pallas_call(functools.partial(relax_kernel, sizes), out_shape=(jax.Sha...  17.5 us
    pallas_call x1, Pallas kernels, shards(): pl.pallas_call(deposit_kernel, out_shape=(jax.ShapeDtypeStruct((4, NZ, CX...  8.43 us
    unnamed x8, local copies, waits for them, and re-layouts  3.86 us

profile of v2, /device:TPU:0, one launch (start us, length us, event | category | flops | bytes accessed | tf_op | source)
XLA Modules:
  0.0 30.5 jit_solution(12209630571323680354)
XLA Ops:
  0.6 0.0 copy-start
  0.6 0.9 %copy-done = f32[4,16384]{1,0:T(4,128)S(1)} copy-done((f32[4,16384]{1,0:T(4,128)S(1)}, f32[4,16384]{1,0:T(4,128)}, u32[]{:S(2)}) %copy-start) | copy-done | bytes 262168
  1.6 0.0 copy-start.1
  1.6 0.9 %copy-done.1 = s32[3,16384]{1,0:T(4,128)S(1)} copy-done((s32[3,16384]{1,0:T(4,128)S(1)}, s32[3,16384]{1,0:T(4,128)}, u32[]{:S(2)}) %copy-start.1) | copy-done | bytes 196632
  2.5 0.0 copy-start.2
  2.5 0.7 %copy-done.2 = s32[1,9]{1,0:T(1,128)S(1)} copy-done((s32[1,9]{1,0:T(1,128)S(1)}, s32[1,9]{1,0:T(1,128)}, u32[]{:S(2)}) %copy-start.2) | copy-done | bytes 60
  3.2 8.4 %deposit.1 = (f32[4,8,16,128]{3,2,1,0:T(8,128)S(1)}, f32[2,4,16,128]{3,2,1,0:T(8,128)S(1)}, f32[2,4,16,128]{3,2,1,0:T(8,128)S(1)}, f32[4,8,128]{2,1,0:T(8,128)S(1)}) custom-call(s32[1,9]{1,0:T(1,128)S(1)} %copy-done.2, f32[4,16384]{1,0:T(4,128)S(1)} %copy-done, s32[3,16384]{1,0:T(4,128)S(1)} %copy-done.1), custom_call_target="tpu_custom_call" | custom-call | tf_op jit(solution)/shard_map/deposit/pallas_call | solution.py:287
  11.6 17.5 %relax.1 = (f32[8,16,128]{2,1,0:T(8,128)S(1)}, f32[3,8,16,128]{3,2,1,0:T(8,128)S(1)}) custom-call(f32[4,8,16,128]{3,2,1,0:T(8,128)S(1)} %get-tuple-element.6.main, f32[2,4,16,128]{3,2,1,0:T(8,128)S(1)} %get-tuple-element.7.xs, f32[2,4,16,128]{3,2,1,0:T(8,128)S(1)} %get-tuple-element.8.ys, f32[4,8,128]{2,1,0:T(8,128)S(1)} %get-tuple-element.9.cs), custom_call_target="tpu_custom_call" | custom-call | tf_op jit(solution)/shard_map/relax/pallas_call | solution.py:304
  29.2 0.6 %copy.7 = f32[8,16,128]{2,1,0:T(8,128)} copy(f32[8,16,128]{2,1,0:T(8,128)S(1)} %get-tuple-element.12) | data formatting | bytes 131072
  29.8 0.7 %copy.8 = f32[3,8,16,128]{3,2,1,0:T(8,128)} copy(f32[3,8,16,128]{3,2,1,0:T(8,128)S(1)} %get-tuple-element.13) | data formatting | bytes 393216
Async XLA Ops:
  0.6 1.0 %copy-start = (f32[4,16384]{1,0:T(4,128)S(1)}, f32[4,16384]{1,0:T(4,128)}, u32[]{:S(2)}) copy-start(f32[4,16384]{1,0:T(4,128)} %payload.1) | copy-start | bytes 786436
  1.6 0.9 %copy-start.1 = (s32[3,16384]{1,0:T(4,128)S(1)}, s32[3,16384]{1,0:T(4,128)}, u32[]{:S(2)}) copy-start(s32[3,16384]{1,0:T(4,128)} %cells.1) | copy-start | bytes 589828
  2.5 0.7 %copy-start.2 = (s32[1,9]{1,0:T(1,128)S(1)}, s32[1,9]{1,0:T(1,128)}, u32[]{:S(2)}) copy-start(s32[1,9]{1,0:T(1,128)} %counts.1) | copy-start | bytes 112

commit v3 on v2

--- a/solution.py
+++ b/solution.py
@@ -29,9 +29,17 @@
 
 
 def deposit_kernel(
-    counts, payload, cells, main, xs, ys, cs, stay_acc, leave_acc
+    counts_hbm, payload_hbm, cells_hbm, main, xs, ys, cs,
+    stay_acc, leave_acc, counts, payload, cells, sems,
 ):
     part = payload.shape[1]
+    copies = [
+        pltpu.make_async_copy(counts_hbm, counts, sems.at[0]),
+        pltpu.make_async_copy(cells_hbm, cells, sems.at[1]),
+        pltpu.make_async_copy(payload_hbm, payload, sems.at[2]),
+    ]
+    for copy in copies:
+        copy.start()
     stay_acc[...] = jnp.zeros_like(stay_acc)
     leave_acc[...] = jnp.zeros_like(leave_acc)
     bf16 = jnp.bfloat16
@@ -40,6 +48,8 @@
     ids = [jnp.concatenate([v] * (BLOCK // 128), axis=1) for v in ids]
     one = jnp.ones((16, BLOCK), bf16)
     none = jnp.zeros((16, BLOCK), bf16)
+    for copy in copies:
+        copy.wait()
     limits = []
     total = jnp.int32(0)
     for e in range(8):
@@ -292,15 +302,19 @@
             jax.ShapeDtypeStruct((2, 4, CX, CY), f32),
             jax.ShapeDtypeStruct((4, 8, CY), f32),
         ),
-        in_specs=[pl.BlockSpec(memory_space=pltpu.SMEM), vmem, vmem],
+        in_specs=[pl.BlockSpec(memory_space=pltpu.HBM)] * 3,
         out_specs=(vmem,) * 4,
         scratch_shapes=[
             pltpu.VMEM((8 * STAY, 2 * CY), f32),
             pltpu.VMEM((8 * LEAVE, 2 * CY), f32),
+            pltpu.SMEM(counts.shape, jnp.int32),
+            pltpu.VMEM(payload.shape, f32),
+            pltpu.VMEM(cells.shape, jnp.int32),
+            pltpu.SemaphoreType.DMA((3,)),
         ],
         compiler_params=pltpu.CompilerParams(vmem_limit_bytes=40 * 1024 * 1024),
         name="deposit",
-    )(counts, payload, cells)
+    )(*[pltpu.with_memory_space_constraint(a, pltpu.HBM) for a in (counts, payload, cells)])
     field, momentum = pl.pallas_call(
         functools.partial(relax_kernel, sizes),
         out_shape=(

time: 30.7 us -> 28.5 us (0.928)
  local copies, waits for them, and re-layouts: 3.86 us -> 1.31 us
  Pallas kernels: 26 us -> 26.4 us
    unnamed x8 -> x2, local copies, waits for them, and re-layouts: 3.86 us -> 1.31 us
    pallas_call x1, Pallas kernels: 8.43 us -> 8.96 us  [shards(): pl.pallas_call(deposit_kernel, out_shape=(jax.ShapeDtypeStruct((4, NZ, CX...]
where the time goes in v3:
time: 28.5 us; the launch traced here: 28.4 us
  Pallas kernels  26.4 us (93%)
  local copies, waits for them, and re-layouts  1.31 us (5%)
  between operations  0.65 us (2%)
    pallas_call x1, Pallas kernels, shards(): pl.pallas_call(functools.partial(relax_kernel, sizes), out_shape=(jax.Sha...  17.5 us
    pallas_call x1, Pallas kernels, shards(): pl.pallas_call(deposit_kernel, out_shape=(jax.ShapeDtypeStruct((4, NZ, CX...  8.96 us
    unnamed x2, local copies, waits for them, and re-layouts  1.31 us

profile of v3, /device:TPU:0, one launch (start us, length us, event | category | flops | bytes accessed | tf_op | source)
XLA Modules:
  0.0 28.4 jit_solution(6495384374202710679)
XLA Ops:
  0.6 9.0 %deposit.1 = (f32[4,8,16,128]{3,2,1,0:T(8,128)S(1)}, f32[2,4,16,128]{3,2,1,0:T(8,128)S(1)}, f32[2,4,16,128]{3,2,1,0:T(8,128)S(1)}, f32[4,8,128]{2,1,0:T(8,128)S(1)}) custom-call(s32[1,9]{1,0:T(1,128)} %counts_hbm.1, f32[4,16384]{1,0:T(4,128)} %payload_hbm.1, s32[3,16384]{1,0:T(4,128)} %cells_hbm.1), custom_call_target="tpu_custom_call" | custom-call | tf_op jit(solution)/shard_map/deposit/pallas_call | solution.py:297
  9.6 17.5 %relax.1 = (f32[8,16,128]{2,1,0:T(8,128)S(1)}, f32[3,8,16,128]{3,2,1,0:T(8,128)S(1)}) custom-call(f32[4,8,16,128]{3,2,1,0:T(8,128)S(1)} %get-tuple-element.6.main, f32[2,4,16,128]{3,2,1,0:T(8,128)S(1)} %get-tuple-element.7.xs, f32[2,4,16,128]{3,2,1,0:T(8,128)S(1)} %get-tuple-element.8.ys, f32[4,8,128]{2,1,0:T(8,128)S(1)} %get-tuple-element.9.cs), custom_call_target="tpu_custom_call" | custom-call | tf_op jit(solution)/shard_map/relax/pallas_call | solution.py:318
  27.1 0.6 %copy.7 = f32[8,16,128]{2,1,0:T(8,128)} copy(f32[8,16,128]{2,1,0:T(8,128)S(1)} %get-tuple-element.12) | data formatting | bytes 131072
  27.7 0.7 %copy.8 = f32[3,8,16,128]{3,2,1,0:T(8,128)} copy(f32[3,8,16,128]{3,2,1,0:T(8,128)S(1)} %get-tuple-element.13) | data formatting | bytes 393216

commit v4 on v3

--- a/solution.py
+++ b/solution.py
@@ -14,7 +14,7 @@
 MX = 2
 MY = 16
 HALO = 8
-BLOCK = 1024
+BLOCK = 2048
 STAY = 64
 LEAVE = 48
 

time: 28.5 us -> 27 us (0.947)
  Pallas kernels: 26.4 us -> 24.9 us
    pallas_call x1, Pallas kernels: 8.96 us -> 7.42 us  [shards(): pl.pallas_call(deposit_kernel, out_shape=(jax.ShapeDtypeStruct((4, NZ, CX...]
where the time goes in v4:
time: 27 us; the launch traced here: 26.9 us
  Pallas kernels  24.9 us (92%)
  local copies, waits for them, and re-layouts  1.31 us (5%)
  between operations  0.65 us (2%)
    pallas_call x1, Pallas kernels, shards(): pl.pallas_call(functools.partial(relax_kernel, sizes), out_shape=(jax.Sha...  17.5 us
    pallas_call x1, Pallas kernels, shards(): pl.pallas_call(deposit_kernel, out_shape=(jax.ShapeDtypeStruct((4, NZ, CX...  7.42 us
    unnamed x2, local copies, waits for them, and re-layouts  1.31 us

profile of v4, /device:TPU:0, one launch (start us, length us, event | category | flops | bytes accessed | tf_op | source)
XLA Modules:
  0.0 26.9 jit_solution(13508818430790039004)
XLA Ops:
  0.6 7.4 %deposit.1 = (f32[4,8,16,128]{3,2,1,0:T(8,128)S(1)}, f32[2,4,16,128]{3,2,1,0:T(8,128)S(1)}, f32[2,4,16,128]{3,2,1,0:T(8,128)S(1)}, f32[4,8,128]{2,1,0:T(8,128)S(1)}) custom-call(s32[1,9]{1,0:T(1,128)} %counts_hbm.1, f32[4,16384]{1,0:T(4,128)} %payload_hbm.1, s32[3,16384]{1,0:T(4,128)} %cells_hbm.1), custom_call_target="tpu_custom_call" | custom-call | tf_op jit(solution)/shard_map/deposit/pallas_call | solution.py:297
  8.1 17.5 %relax.1 = (f32[8,16,128]{2,1,0:T(8,128)S(1)}, f32[3,8,16,128]{3,2,1,0:T(8,128)S(1)}) custom-call(f32[4,8,16,128]{3,2,1,0:T(8,128)S(1)} %get-tuple-element.6.main, f32[2,4,16,128]{3,2,1,0:T(8,128)S(1)} %get-tuple-element.7.xs, f32[2,4,16,128]{3,2,1,0:T(8,128)S(1)} %get-tuple-element.8.ys, f32[4,8,128]{2,1,0:T(8,128)S(1)} %get-tuple-element.9.cs), custom_call_target="tpu_custom_call" | custom-call | tf_op jit(solution)/shard_map/relax/pallas_call | solution.py:318
  25.5 0.6 %copy.7 = f32[8,16,128]{2,1,0:T(8,128)} copy(f32[8,16,128]{2,1,0:T(8,128)S(1)} %get-tuple-element.12) | data formatting | bytes 131072
  26.2 0.7 %copy.8 = f32[3,8,16,128]{3,2,1,0:T(8,128)} copy(f32[3,8,16,128]{3,2,1,0:T(8,128)S(1)} %get-tuple-element.13) | data formatting | bytes 393216

commit v5 on v4

--- a/solution.py
+++ b/solution.py
@@ -14,7 +14,7 @@
 MX = 2
 MY = 16
 HALO = 8
-BLOCK = 2048
+BLOCK = 4096
 STAY = 64
 LEAVE = 48
 

time: 27 us -> 26.7 us (0.989)
  Pallas kernels: 24.9 us -> 24.5 us
    pallas_call x1, Pallas kernels: 7.42 us -> 7.07 us  [shards(): pl.pallas_call(deposit_kernel, out_shape=(jax.ShapeDtypeStruct((4, NZ, CX...]
where the time goes in v5:
time: 26.7 us; the launch traced here: 26.5 us
  Pallas kernels  24.5 us (92%)
  local copies, waits for them, and re-layouts  1.31 us (5%)
  between operations  0.65 us (2%)
    pallas_call x1, Pallas kernels, shards(): pl.pallas_call(functools.partial(relax_kernel, sizes), out_shape=(jax.Sha...  17.5 us
    pallas_call x1, Pallas kernels, shards(): pl.pallas_call(deposit_kernel, out_shape=(jax.ShapeDtypeStruct((4, NZ, CX...  7.07 us
    unnamed x2, local copies, waits for them, and re-layouts  1.31 us

profile of v5, /device:TPU:0, one launch (start us, length us, event | category | flops | bytes accessed | tf_op | source)
XLA Modules:
  0.0 26.5 jit_solution(12313468918919303917)
XLA Ops:
  0.6 7.1 %deposit.1 = (f32[4,8,16,128]{3,2,1,0:T(8,128)S(1)}, f32[2,4,16,128]{3,2,1,0:T(8,128)S(1)}, f32[2,4,16,128]{3,2,1,0:T(8,128)S(1)}, f32[4,8,128]{2,1,0:T(8,128)S(1)}) custom-call(s32[1,9]{1,0:T(1,128)} %counts_hbm.1, f32[4,16384]{1,0:T(4,128)} %payload_hbm.1, s32[3,16384]{1,0:T(4,128)} %cells_hbm.1), custom_call_target="tpu_custom_call" | custom-call | tf_op jit(solution)/shard_map/deposit/pallas_call | solution.py:297
  7.7 17.5 %relax.1 = (f32[8,16,128]{2,1,0:T(8,128)S(1)}, f32[3,8,16,128]{3,2,1,0:T(8,128)S(1)}) custom-call(f32[4,8,16,128]{3,2,1,0:T(8,128)S(1)} %get-tuple-element.6.main, f32[2,4,16,128]{3,2,1,0:T(8,128)S(1)} %get-tuple-element.7.xs, f32[2,4,16,128]{3,2,1,0:T(8,128)S(1)} %get-tuple-element.8.ys, f32[4,8,128]{2,1,0:T(8,128)S(1)} %get-tuple-element.9.cs), custom_call_target="tpu_custom_call" | custom-call | tf_op jit(solution)/shard_map/relax/pallas_call | solution.py:318
  25.2 0.6 %copy.7 = f32[8,16,128]{2,1,0:T(8,128)} copy(f32[8,16,128]{2,1,0:T(8,128)S(1)} %get-tuple-element.12) | data formatting | bytes 131072
  25.8 0.7 %copy.8 = f32[3,8,16,128]{3,2,1,0:T(8,128)} copy(f32[3,8,16,128]{3,2,1,0:T(8,128)S(1)} %get-tuple-element.13) | data formatting | bytes 393216
